TPU v7x, 512 devices: a whole 4x4x16 slice. The times are simulated.
512 devices in a mesh: row: 64 (over z, y), grp: 8 (over x, core).
Axes of the slice: x: 4, y: 4, z: 16, core: 2. Of those that a mesh axis runs over, the one named last changes fastest.
Arguments:
- design: float32 [131072, 2048], P('row', 'grp')
- rademacher: int32 [131072], P('row'), may hold values from 0 to 1
- target: float32 [131072], P('row'), may hold values from -6 to 6
- sample_rows: int32 [64, 8, 16], P('row', 'grp'), may hold values from 0 to 2047
- checksum_seeds: int32 [2048], P('grp'), may hold values from 1 to 16
Outputs:
- solution: float32 [2048], P('grp')
- residual: float32 [131072], P('row')
- checksum: float32 [2048], P('grp')
Inputs may be any that keep to these rules, and one draw needn't show every extreme that they name: sample_rows holds row numbers within one index's block of 2048 rows; a row may be drawn more than once.
All inputs are finite; a program needn't handle non-finite values.
Results may differ from a plain program's by a relative error of at most 0.0003.
Values sent between devices are 32-bit elements; how exact they have to be, the bound alone decides.
No kernel may reach another device: no remote copies, remote signals or barrier semaphores. Data moves between devices by JAX's collectives and lax.ppermute only.
A program may use at most 64 MiB of HBM per device.

v0:
```python
import functools

import jax
import jax.numpy as jnp
from jax import lax
from jax.experimental import pallas as pl
from jax.experimental.pallas import tpu as pltpu
from jax.sharding import Mesh, PartitionSpec as P

ZB, ZA, Y, X, C = 8, 2, 4, 4, 2
SOURCES = ZB * ZA * Y
FAR = "zb"
NEAR = ("za", "y")
ROWS = (FAR,) + NEAR
GRPS = ("x", "c")
F32 = jnp.float32
BF16 = jnp.bfloat16
VMEM = pl.BlockSpec(memory_space=pltpu.VMEM)
SMEM = pl.BlockSpec(memory_space=pltpu.SMEM)


def cost(flops, size):
    return pl.CostEstimate(flops=flops, bytes_accessed=size, transcendentals=0)


def parity_sign(bits):
    bits = jnp.bitwise_xor(bits, jnp.right_shift(bits, 8))
    bits = jnp.bitwise_xor(bits, jnp.right_shift(bits, 4))
    odd = jnp.bitwise_and(jnp.right_shift(0x6996, jnp.bitwise_and(bits, 15)), 1)
    return 1.0 - 2.0 * odd.astype(F32)


def split3(value):
    hi = value.astype(BF16)
    rest = value - hi.astype(F32)
    mid = rest.astype(BF16)
    lo = (rest - mid.astype(F32)).astype(BF16)
    return hi, mid, lo


def mix_kernel(tgt_ref, rad_ref, slab_ref, mixed_ref, back_ref, work_ref):
    height, breadth = slab_ref.shape
    block = 256
    blocks = height // block
    row = lax.broadcasted_iota(jnp.int32, (block, block), 0)
    lane = lax.broadcasted_iota(jnp.int32, (block, block), 1)
    table = parity_sign(jnp.bitwise_and(row, lane)) * 0.03125
    rows = jnp.concatenate(list(split3(tgt_ref[...])) + [jnp.zeros((13, height), BF16)], axis=0)
    back = jnp.zeros((16, breadth), F32)
    for place in range(blocks):
        at = place * block
        sign = 1.0 - 2.0 * rad_ref[:, at : at + block].astype(F32)
        left = (table * sign).astype(BF16)
        total = jnp.zeros((block, breadth), F32)
        for term in split3(slab_ref[at : at + block, :]):
            total = total + jnp.dot(left, term, preferred_element_type=F32)
            back = back + jnp.dot(rows[:, at : at + block], term, preferred_element_type=F32)
        work_ref[at : at + block, :] = total
    back = jnp.sum(back, axis=0, keepdims=True)
    for copy in range(4):
        back_ref[2 * copy : 2 * copy + 1, :] = back[:, :128]
        back_ref[2 * copy + 1 : 2 * copy + 2, :] = back[:, 128:]
    for chunk in range(block // 8):
        tiles = [work_ref[b * block + chunk * 8 : b * block + chunk * 8 + 8, :] for b in range(blocks)]
        stride = 1
        while stride < blocks:
            tiles = [
                tiles[b] + tiles[b ^ stride] if b & stride == 0 else tiles[b ^ stride] - tiles[b]
                for b in range(blocks)
            ]
            stride *= 2
        for b in range(blocks):
            at = 2 * (b * block + chunk * 8)
            mixed_ref[pl.ds(at, 8, stride=2), :] = tiles[b][:, :128]
            mixed_ref[pl.ds(at + 1, 8, stride=2), :] = tiles[b][:, 128:]


def mix(target, rademacher, design):
    height, breadth = design.shape
    return pl.pallas_call(
        mix_kernel,
        out_shape=(
            jax.ShapeDtypeStruct((2 * height, 128), F32),
            jax.ShapeDtypeStruct((8, 128), F32),
        ),
        in_specs=[VMEM] * 3,
        out_specs=(VMEM,) * 2,
        scratch_shapes=[pltpu.VMEM((height, breadth), F32)],
        compiler_params=pltpu.CompilerParams(vmem_limit_bytes=24 * 2**20),
        cost_estimate=cost(2**30, 2**23),
        name="mix",
    )(target, rademacher, design)


def pick_kernel(pos_ref, idx_ref, mixed_ref, back_ref, out_ref):
    per_owner = idx_ref.shape[2]
    owners = 128 // per_owner

    def one(piece, carry):
        for near in range(owners):
            owner = piece * owners + near
            odd = jnp.bitwise_and(owner, pos_ref[0])
            for shift in (4, 2, 1):
                odd = jnp.bitwise_xor(odd, jnp.right_shift(odd, shift))
            sign = (1 - 2 * jnp.bitwise_and(odd, 1)).astype(F32)
            for slot in range(per_owner):
                drawn = mixed_ref[idx_ref[owner, 0, slot]]
                out_ref[piece, near * per_owner + slot] = drawn * sign
        out_ref[piece, 128:132] = back_ref[...]
        return carry

    lax.fori_loop(0, out_ref.shape[0], one, 0)


def pick(position, drawn, mixed, back):
    return pl.pallas_call(
        pick_kernel,
        out_shape=jax.ShapeDtypeStruct((ZA * Y, 132, 2, 128), F32),
        in_specs=[SMEM] * 2 + [VMEM] * 2,
        out_specs=VMEM,
        compiler_params=pltpu.CompilerParams(vmem_limit_bytes=8 * 2**20),
        cost_estimate=cost(2**20, 2**21),
        name="pick",
    )(position, drawn, mixed, back)


def exchange(pieces, axes):
    return lax.all_to_all(pieces, axes, split_axis=0, concat_axis=0, tiled=True)


def share(value, axes, count):
    return exchange(jnp.broadcast_to(value[None], (count,) + value.shape), axes)


NB = 32


def spread_row(value, row):
    return jnp.broadcast_to(value[row : row + 1, :], (8, value.shape[1]))


def dot_nt(left, right):
    return lax.dot_general(left, right, (((1,), (1,)), ((), ())), preferred_element_type=F32)


def dot_tn(left, right):
    return lax.dot_general(left, right, (((0,), (0,)), ((), ())), preferred_element_type=F32)


def deal_kernel(parts_ref, out_ref):
    total = jnp.sum(parts_ref[...], axis=0)
    for copy in range(ZB):
        out_ref[copy, 0:32, :] = total[32 * copy : 32 * copy + 32]
        out_ref[copy, 32:40, :] = total[256:264]


def deal(parts):
    return pl.pallas_call(
        deal_kernel,
        out_shape=jax.ShapeDtypeStruct((ZB, 40, 128), F32),
        in_specs=[VMEM],
        out_specs=VMEM,
        compiler_params=pltpu.CompilerParams(vmem_limit_bytes=8 * 2**20),
        name="deal",
    )(parts)


def fold_kernel(parts_ref, rows_ref, back_ref):
    total = jnp.sum(parts_ref[...], axis=0)
    for copy in range(ZB):
        rows_ref[copy] = total[0:32]
    back_ref[:, 0:128] = total[32:33]
    back_ref[:, 128:256] = total[33:34]


def fold(parts):
    return pl.pallas_call(
        fold_kernel,
        out_shape=(
            jax.ShapeDtypeStruct((ZB, 32, 128), F32),
            jax.ShapeDtypeStruct((1, 256), F32),
        ),
        in_specs=[VMEM],
        out_specs=(VMEM,) * 2,
        compiler_params=pltpu.CompilerParams(vmem_limit_bytes=4 * 2**20),
        name="fold",
    )(parts)


def gram_products(rows):
    hi, mid, lo = split3(rows)
    right = jnp.concatenate([hi, mid, hi, lo, hi, mid], axis=0)
    hi, mid, lo = split3(rows.T)
    left = jnp.concatenate([hi, hi, mid, hi, lo, mid], axis=1)
    top = jnp.dot(left[:128], right, preferred_element_type=F32)
    end = jnp.dot(left[128:], right[:, 128:], preferred_element_type=F32)
    return top[:, :128], top[:, 128:], end


def gram_kernel(rows_ref, out_ref):
    count = rows_ref.shape[0] // 2
    rows = [rows_ref[pl.ds(half, count, stride=2), :] for half in range(2)]
    first, corner, last = gram_products(jnp.concatenate(rows, axis=1))
    row = lax.broadcasted_iota(jnp.int32, (128, 128), 0)
    lane = lax.broadcasted_iota(jnp.int32, (128, 128), 1)
    mixed = jnp.where(row <= lane, first, last)
    diagonal = jnp.sum(jnp.where(row == lane, last, 0.0), axis=0, keepdims=True)
    for copy in range(ZA * Y):
        out_ref[copy, 0:128, :] = mixed
        out_ref[copy, 128:256, :] = corner
        out_ref[copy, 256:264, :] = jnp.broadcast_to(diagonal, (8, 128))


def gram(rows):
    return pl.pallas_call(
        gram_kernel,
        out_shape=jax.ShapeDtypeStruct((ZA * Y, 264, 128), F32),
        in_specs=[VMEM],
        out_specs=VMEM,
        cost_estimate=cost(2**27, 2**20),
        compiler_params=pltpu.CompilerParams(vmem_limit_bytes=4 * 2**20),
        name="gram",
    )(rows)


def factor_kernel(gram_ref, back_ref, seed_ref, slab_ref, image_ref, dir_ref, check_ref, work_ref):
    height, size = slab_ref.shape
    blocks = jnp.sum(gram_ref[...], axis=0)
    mixed, corner, diagonal = blocks[:128], blocks[128:256], blocks[256:257]
    turned = mixed.T
    row = lax.broadcasted_iota(jnp.int32, (128, 128), 0)
    lane = lax.broadcasted_iota(jnp.int32, (128, 128), 1)
    first = jnp.where(row <= lane, mixed, turned)
    last = jnp.where(row == lane, diagonal, jnp.where(row > lane, mixed, turned))
    gram = jnp.concatenate(
        [
            jnp.concatenate([first, corner], axis=1),
            jnp.concatenate([corner.T, last], axis=1),
        ],
        axis=0,
    )
    sub = lax.broadcasted_iota(jnp.int32, (128, size), 0)
    weights = seed_ref[...].astype(F32) * 0.0625
    weight_rows = jnp.where(sub == 1, jnp.broadcast_to(weights, (128, size)), 0.0).astype(BF16)
    back_rows = jnp.where(sub == 0, jnp.broadcast_to(back_ref[...], (128, size)), 0.0)
    eye = (
        lax.broadcasted_iota(jnp.int32, (size, size), 0)
        == lax.broadcasted_iota(jnp.int32, (size, size), 1)
    ).astype(BF16)
    extra = jnp.zeros((size, 128), F32)
    for term in split3(gram):
        extra = extra + dot_nt(term, weight_rows)
    for term in split3(back_rows):
        extra = extra + dot_nt(eye, term)
    work_ref[:, :size] = gram
    work_ref[:, size:] = extra

    wide = size + 128
    lane = lax.broadcasted_iota(jnp.int32, (NB, wide), 1)
    row = lax.broadcasted_iota(jnp.int32, (NB, wide), 0)
    half_row = lax.broadcasted_iota(jnp.int32, (8, 128), 0)
    wide_half = lax.broadcasted_iota(jnp.int32, (8, wide), 1)
    half_count = NB // 8
    tiles = wide // 128
    for block in range(size // NB):
        at = block * NB
        halves = [work_ref[at + 8 * h : at + 8 * h + 8, :] for h in range(half_count)]
        scales = [jnp.zeros((8, 128), F32)] * half_count
        for phase in range(2):
            base = 16 * phase
            begin = at + base
            cols = {
                (c, h): jnp.broadcast_to(halves[h][:, at + c : at + c + 1], (8, 128))
                for c in range(base, base + 16)
                for h in range(c // 8, half_count)
            }
            for h in range(2 * phase, half_count):
                unit = (wide_half - begin == half_row[:, :1] + (8 * h - base)).astype(F32)
                inside = (wide_half >= begin) & (wide_half < begin + 16)
                halves[h] = jnp.where(inside, unit, halves[h])
            pivot = spread_row(cols[base, base // 8], 0)
            for j in range(base, base + 16):
                inverse = pl.reciprocal(pivot, approx=True)
                for _ in range(2):
                    inverse = inverse * (2.0 - pivot * inverse)
                here = j // 8
                scales[here] = jnp.where(half_row == j % 8, pivot, scales[here])
                if j + 1 == NB:
                    break
                across = {
                    c: spread_row(cols[j, c // 8], c % 8) for c in range(j + 1, base + 16)
                }
                if j + 1 < base + 16:
                    pivot = (
                        spread_row(cols[j + 1, (j + 1) // 8], (j + 1) % 8)
                        - across[j + 1] * across[j + 1] * inverse
                    )
                source = jnp.tile(inverse, (1, tiles)) * spread_row(halves[here], j % 8)
                for h in range((j + 1) // 8, half_count):
                    below = cols[j, h]
                    if h == here:
                        below = jnp.where(half_row > j % 8, below, 0.0)
                    halves[h] = halves[h] - jnp.tile(below, (1, tiles)) * source
                    for c in range(j + 1, base + 16):
                        if c // 8 <= h:
                            cols[c, h] = cols[c, h] - below * (across[c] * inverse)
        panel = jnp.concatenate(
            [
                half * jnp.tile(lax.rsqrt(scale), (1, tiles))
                for half, scale in zip(halves, scales)
            ],
            axis=0,
        )
        work_ref[at : at + NB, :] = panel
        if at + NB < size:
            hi, mid, lo = split3(panel)
            zero = jnp.zeros((NB, size), BF16)
            keep = lane[:, :size] >= at + NB
            lhi, lmid, llo = [jnp.where(keep, term[:, :size], zero) for term in (hi, mid, lo)]
            left = jnp.concatenate([lhi, lhi, lmid, lhi, llo, lmid], axis=0)
            blank = (row < 16) & (lane >= at + 16) & (lane < at + NB)
            hi, mid, lo = [
                jnp.where(blank, jnp.zeros((NB, wide), BF16), term) for term in (hi, mid, lo)
            ]
            right = jnp.concatenate([hi, mid, hi, lo, hi, mid], axis=0)
            change = dot_tn(left, right)
            rest = size - at - NB
            wide_lane = lax.broadcasted_iota(jnp.int32, (rest, wide), 1)
            old = work_ref[at + NB :, :]
            old = jnp.where((wide_lane >= at) & (wide_lane < at + NB), 0.0, old)
            work_ref[at + NB :, :] = old - change[at + NB :, :]

    lower_inv = jnp.where(
        lax.broadcasted_iota(jnp.int32, (size, size), 0)
        >= lax.broadcasted_iota(jnp.int32, (size, size), 1),
        work_ref[:, :size],
        0.0,
    )
    half = work_ref[:, size : size + 1]
    check = work_ref[:, size + 1 : size + 2]
    direction = jnp.sum(lower_inv * half, axis=0, keepdims=True)
    diagonal = eye.astype(F32)
    check_ref[...] = jnp.sum(diagonal * check, axis=0, keepdims=True)
    dir_ref[...] = direction
    energy = jnp.sum(half * half, axis=0, keepdims=True)

    dhi, dmid, dlo = split3(direction)
    rows = jnp.concatenate([dhi, dmid, dlo, jnp.zeros((13, size), BF16)], axis=0)
    for part in range(height // 256):
        total = jnp.zeros((16, 256), F32)
        for term in split3(slab_ref[part * 256 : (part + 1) * 256, :]):
            total = total + dot_nt(rows, term)
        image = jnp.sum(total, axis=0, keepdims=True)
        for half in range(2):
            at = 2 * part + half
            image_ref[:, at : at + 1, :] = jnp.broadcast_to(
                image[None, :, half * 128 : (half + 1) * 128], (X * C, 1, 128)
            )
    image_ref[:, height // 128 :, :] = jnp.broadcast_to(energy[None], (X * C, 8, 128))


def factor(grams, back, seeds, design):
    height, breadth = design.shape
    return pl.pallas_call(
        factor_kernel,
        out_shape=(
            jax.ShapeDtypeStruct((X * C, height // 128 + 8, 128), F32),
            jax.ShapeDtypeStruct((1, breadth), F32),
            jax.ShapeDtypeStruct((1, breadth), F32),
        ),
        in_specs=[VMEM] * 4,
        out_specs=(VMEM,) * 3,
        scratch_shapes=[pltpu.VMEM((breadth, breadth + 128), F32)],
        compiler_params=pltpu.CompilerParams(vmem_limit_bytes=40 * 2**20),
        cost_estimate=cost(2**29, 2**22),
        name="factor",
    )(grams, back, seeds, design)


def merge_kernel(parts_ref, image_ref, energy_ref):
    image = jnp.sum(parts_ref[...], axis=0)
    image_ref[...] = image
    squares = jnp.sum(image[:-8] * image[:-8], axis=0, keepdims=True)
    energy = jnp.sum(squares, axis=1, keepdims=True)
    energy_ref[...] = jnp.broadcast_to(energy.reshape(1, 1, 1), energy_ref.shape)


def merge(parts):
    return pl.pallas_call(
        merge_kernel,
        out_shape=(
            jax.ShapeDtypeStruct(parts.shape[1:], F32),
            jax.ShapeDtypeStruct((SOURCES, 1, 128), F32),
        ),
        in_specs=[VMEM],
        out_specs=(VMEM,) * 2,
        compiler_params=pltpu.CompilerParams(vmem_limit_bytes=4 * 2**20),
        name="merge",
    )(parts)


def finish_kernel(energy_ref, image_ref, tgt_ref, dir_ref, sol_ref, res_ref):
    height = tgt_ref.shape[0]
    step = image_ref[height : height + 1, :] / jnp.sum(energy_ref[...], axis=0)
    sol_ref[...] = jnp.tile(step, (1, dir_ref.shape[1] // 128)) * dir_ref[...]
    res_ref[...] = tgt_ref[...] - step * image_ref[:height]


def finish(energies, image, target, direction):
    return pl.pallas_call(
        finish_kernel,
        out_shape=(
            jax.ShapeDtypeStruct(direction.shape, F32),
            jax.ShapeDtypeStruct(target.shape, F32),
        ),
        in_specs=[VMEM] * 4,
        out_specs=(VMEM,) * 2,
        compiler_params=pltpu.CompilerParams(vmem_limit_bytes=4 * 2**20),
        name="finish",
    )(energies, image, target, direction)


def body(design, rademacher, target, sample_rows, checksum_seeds):
    height, breadth = design.shape
    position = lax.axis_index(ROWS).astype(jnp.int32).reshape(1)
    drawn = share(sample_rows.reshape(1, 16), ROWS, SOURCES)
    mixed, back = mix(target.reshape(1, height), rademacher.reshape(1, height), design)
    near = pick(position, drawn, mixed.reshape(height, 2, 128), back.reshape(4, 2, 128))
    pieces = deal(exchange(near.reshape(ZA * Y, 264, 128), NEAR))
    rows, back = fold(exchange(pieces, FAR))
    rows = exchange(rows, FAR).reshape(ZB * 32, 128)
    images, direction, checksum = factor(
        exchange(gram(rows), NEAR), back, checksum_seeds.reshape(1, breadth), design
    )
    image, energy = merge(exchange(images, GRPS))
    solved, residual = finish(
        exchange(energy, ROWS), image, target.reshape(height // 128, 128), direction
    )
    return solved.reshape(breadth), residual.reshape(height), checksum.reshape(breadth)


def solution(mesh):
    fine = Mesh(mesh.devices.reshape(ZB, ZA, Y, X, C), ROWS + GRPS)
    in_specs = (P(ROWS, GRPS), P(ROWS), P(ROWS), P(ROWS, GRPS, None), P(GRPS))
    out_specs = (P(GRPS), P(ROWS), P(GRPS))
    return jax.shard_map(body, mesh=fine, in_specs=in_specs, out_specs=out_specs, check_vma=False)
```

profile of v0, /device:TPU:1, one launch (start us, length us, event | category | flops | bytes accessed | tf_op | source)
XLA Modules:
  0.0 143.7 jit_solution(6111549241064742162)
XLA Ops:
  0.6 1.3 broadcast_in_dim.8
  1.9 19.3 %all-to-all-start = ((s32[64,1,16]{2,1,0:T(1,128)}), s32[64,1,16]{2,1,0:T(1,128)S(1)}, u32[]{:S(2)}, u32[]{:S(2)}) async-start(s32[64,1,16]{2,1,0:T(1,128)} %broadcast_in_dim.8), calls=%async_computation | async-start | bytes 65536 | tf_op jit(solution)/shard_map/all_to_all | solution.py:128
  21.2 0.0 copy-start
  21.2 1.6 %copy-done = f32[2048,256]{1,0:T(8,128)S(1)} copy-done((f32[2048,256]{1,0:T(8,128)S(1)}, f32[2048,256]{1,0:T(8,128)}, u32[]{:S(2)}) %copy-start) | copy-done | bytes 2097176
  22.8 0.7 copy-done.2
  23.5 0.7 copy-done.5
  24.2 1.6 %mix.1 = (f32[4096,128]{1,0:T(8,128)S(1)}, f32[8,128]{1,0:T(8,128)S(1)}) custom-call(f32[1,2048]{1,0:T(1,128)S(1)} %bitcast.16, s32[1,2048]{1,0:T(1,128)S(1)} %bitcast.20, f32[2048,256]{1,0:T(8,128)S(1)} %copy-done), custom_call_target="tpu_custom_call" | custom-call | flops 1073741824 | bytes 8388608 | tf_op jit(solution)/shard_map/mix/pallas_call | solution.py:80
  25.8 9.0 %all-to-all-done.idx_ref = s32[64,1,16]{2,1,0:T(1,128)S(1)} async-done(((s32[64,1,16]{2,1,0:T(1,128)}), s32[64,1,16]{2,1,0:T(1,128)S(1)}, u32[]{:S(2)}, u32[]{:S(2)}) %all-to-all-start) | async-done | bytes 4128 | tf_op jit(solution)/shard_map/all_to_all | solution.py:128
  34.8 2.4 %pick.1 = f32[8,132,2,128]{3,2,1,0:T(2,128)S(1)} custom-call(s32[1]{0:T(128)} %bitcast.pos_ref, s32[64,1,16]{2,1,0:T(1,128)S(1)} %all-to-all-done.idx_ref, f32[2048,2,128]{2,1,0:T(2,128)S(1)} %bitcast.14, f32[4,2,128]{2,1,0:T(2,128)S(1)} %bitcast.18), custom_call_target="tpu_custom_call" | custom-call | flops 1048576 | bytes 2097152 | tf_op jit(solution)/shard_map/pick/pallas_call | solution.py:116
  37.2 16.4 %all_to_all.35.parts_ref = f32[8,264,128]{2,1,0:T(8,128)S(1)} all-to-all(f32[8,264,128]{2,1,0:T(8,128)S(1)} %bitcast.13), channel_id=1, replica_groups=mesh['zb'=8,'za'=2,'y'=4,'x'=4,'c'=2] {'za','y'}, dimensions={0} | all-to-all | bytes 2162688 | tf_op jit(solution)/shard_map/all_to_all | solution.py:128
  53.6 0.1 deal.1
  53.7 17.8 %all_to_all.36.parts_ref = f32[8,40,128]{2,1,0:T(8,128)S(1)} all-to-all(f32[8,40,128]{2,1,0:T(8,128)S(1)} %deal.1), channel_id=1, replica_groups=mesh['zb'=8,'za'=2,'y'=4,'x'=4,'c'=2] {'zb'}, dimensions={0} | all-to-all | bytes 327680 | tf_op jit(solution)/shard_map/all_to_all | solution.py:128
  71.4 15.6 %all_to_all.37 = f32[8,32,128]{2,1,0:T(8,128)S(1)} all-to-all(f32[8,32,128]{2,1,0:T(8,128)S(1)} %get-tuple-element.16), channel_id=1, replica_groups=mesh['zb'=8,'za'=2,'y'=4,'x'=4,'c'=2] {'zb'}, dimensions={0} | all-to-all | bytes 262144 | tf_op jit(solution)/shard_map/all_to_all | solution.py:128
  87.0 0.3 gram.1
  87.4 0.0 copy-start.1
  87.4 0.0 copy-start.4
  87.4 13.8 %all_to_all.38.gram_ref = f32[8,264,128]{2,1,0:T(8,128)S(1)} all-to-all(f32[8,264,128]{2,1,0:T(8,128)S(1)} %gram.1), channel_id=1, replica_groups=mesh['zb'=8,'za'=2,'y'=4,'x'=4,'c'=2] {'za','y'}, dimensions={0} | all-to-all | bytes 2162688 | tf_op jit(solution)/shard_map/all_to_all | solution.py:128
  101.2 0.0 copy-done.1
  101.2 0.0 copy-done.4
  101.2 8.4 %factor.1 = (f32[8,24,128]{2,1,0:T(8,128)S(1)}, f32[1,256]{1,0:T(1,128)S(1)}, f32[1,256]{1,0:T(1,128)}) custom-call(f32[8,264,128]{2,1,0:T(8,128)S(1)} %all_to_all.38.gram_ref, f32[1,256]{1,0:T(1,128)S(1)} %get-tuple-element.17.back_ref, s32[1,256]{1,0:T(1,128)S(1)} %bitcast.19, f32[2048,256]{1,0:T(8,128)S(1)} %copy-done.1), custom_call_target="tpu_custom_call" | custom-call | flops 536870912 | bytes 4194304 | tf_op jit(solution)/shard_map/factor/pallas_call | solution.py:364
  109.6 15.5 %all_to_all.39.parts_ref = f32[8,24,128]{2,1,0:T(8,128)S(1)} all-to-all(f32[8,24,128]{2,1,0:T(8,128)S(1)} %get-tuple-element.18), channel_id=1, replica_groups=mesh['zb'=8,'za'=2,'y'=4,'x'=4,'c'=2] {'x','c'}, dimensions={0} | all-to-all | bytes 196608 | tf_op jit(solution)/shard_map/all_to_all | solution.py:128
  125.1 0.1 merge.1
  125.2 17.7 %all_to_all.40.energy_ref = f32[64,1,128]{2,1,0:T(1,128)S(1)} all-to-all(f32[64,1,128]{2,1,0:T(1,128)S(1)} %get-tuple-element.19), channel_id=1, replica_groups=mesh['zb'=8,'za'=2,'y'=4,'x'=4,'c'=2] {'zb','za','y'}, dimensions={0} | all-to-all | bytes 65536 | tf_op jit(solution)/shard_map/all_to_all | solution.py:128
  143.0 0.7 finish.1
  (5 shorter events, 0.0 us)
Async XLA Ops:
  1.9 32.9 %all-to-all-start = ((s32[64,1,16]{2,1,0:T(1,128)}), s32[64,1,16]{2,1,0:T(1,128)S(1)}, u32[]{:S(2)}, u32[]{:S(2)}) async-start(s32[64,1,16]{2,1,0:T(1,128)} %broadcast_in_dim.8), calls=%async_computation | async-start | bytes 65536 | tf_op jit(solution)/shard_map/all_to_all | solution.py:128
  21.2 1.6 %copy-start = (f32[2048,256]{1,0:T(8,128)S(1)}, f32[2048,256]{1,0:T(8,128)}, u32[]{:S(2)}) copy-start(f32[2048,256]{1,0:T(8,128)} %slab_ref.3) | copy-start | bytes 6291460
  22.8 0.7 copy-start.2
  23.5 0.7 copy-start.5
  87.4 13.8 %copy-start.1 = (f32[2048,256]{1,0:T(8,128)S(1)}, f32[2048,256]{1,0:T(8,128)}, u32[]{:S(2)}) copy-start(f32[2048,256]{1,0:T(8,128)} %slab_ref.3) | copy-start | bytes 6291460
  87.4 13.8 %copy-start.4 = (s32[256]{0:T(256)S(1)}, s32[256]{0:T(256)}, u32[]{:S(2)}) copy-start(s32[256]{0:T(256)} %param.9) | copy-start | bytes 3076
  101.2 41.8 %copy-start.3 = (f32[2048]{0:T(1024)S(1)}, f32[2048]{0:T(1024)}, u32[]{:S(2)}) copy-start(f32[2048]{0:T(1024)} %param.7) | copy-start | bytes 24580
where the time goes:
time: 144 us
  blocking collectives  96.8 us (67%)
  starting transfers between devices  19.3 us (13%)
  Pallas kernels  13.6 us (9%)
  waiting for transfers between devices  9 us (6%)
  local copies, waits for them, and re-layouts  4.28 us (3%)
    all_to_all x6, blocking collectives, exchange(): return lax.all_to_all(pieces, axes, split_axis=0, concat_axis=0, tiled=True)  96.8 us
    all_to_all x1, starting transfers between devices, exchange(): return lax.all_to_all(pieces, axes, split_axis=0, concat_axis=0, tiled=True)  19.3 us
    all_to_all x1, waiting for transfers between devices, exchange(): return lax.all_to_all(pieces, axes, split_axis=0, concat_axis=0, tiled=True)  9 us
    pallas_call x1, Pallas kernels, factor(): pl.pallas_call(factor_kernel, out_shape=(jax.ShapeDtypeStruct((X * C, hei...  8.4 us
    unnamed x12, local copies, waits for them, and re-layouts  3 us
  transfers between devices with their start and end apart: 1, of which 1 were waited for; matrix products, arithmetic and copies ran while one was open for 0% of the time, Pallas kernels for 1%

commit v1 on v0

--- a/solution.py
+++ b/solution.py
@@ -106,7 +106,7 @@
             for slot in range(per_owner):
                 drawn = mixed_ref[idx_ref[owner, 0, slot]]
                 out_ref[piece, near * per_owner + slot] = drawn * sign
-        out_ref[piece, 128:132] = back_ref[...]
+        out_ref[piece, 128] = back_ref[0]
         return carry
 
     lax.fori_loop(0, out_ref.shape[0], one, 0)
@@ -115,7 +115,7 @@
 def pick(position, drawn, mixed, back):
     return pl.pallas_call(
         pick_kernel,
-        out_shape=jax.ShapeDtypeStruct((ZA * Y, 132, 2, 128), F32),
+        out_shape=jax.ShapeDtypeStruct((ZA * Y, 129, 2, 128), F32),
         in_specs=[SMEM] * 2 + [VMEM] * 2,
         out_specs=VMEM,
         compiler_params=pltpu.CompilerParams(vmem_limit_bytes=8 * 2**20),
@@ -150,14 +150,14 @@
 def deal_kernel(parts_ref, out_ref):
     total = jnp.sum(parts_ref[...], axis=0)
     for copy in range(ZB):
-        out_ref[copy, 0:32, :] = total[32 * copy : 32 * copy + 32]
-        out_ref[copy, 32:40, :] = total[256:264]
+        out_ref[copy, 0:16] = total[16 * copy : 16 * copy + 16]
+        out_ref[copy, 16:17] = total[128:129]
 
 
 def deal(parts):
     return pl.pallas_call(
         deal_kernel,
-        out_shape=jax.ShapeDtypeStruct((ZB, 40, 128), F32),
+        out_shape=jax.ShapeDtypeStruct((ZB, 17, 2, 128), F32),
         in_specs=[VMEM],
         out_specs=VMEM,
         compiler_params=pltpu.CompilerParams(vmem_limit_bytes=8 * 2**20),
@@ -168,17 +168,16 @@
 def fold_kernel(parts_ref, rows_ref, back_ref):
     total = jnp.sum(parts_ref[...], axis=0)
     for copy in range(ZB):
-        rows_ref[copy] = total[0:32]
-    back_ref[:, 0:128] = total[32:33]
-    back_ref[:, 128:256] = total[33:34]
+        rows_ref[copy] = total[0:16]
+    back_ref[...] = total[16:17]
 
 
 def fold(parts):
     return pl.pallas_call(
         fold_kernel,
         out_shape=(
-            jax.ShapeDtypeStruct((ZB, 32, 128), F32),
-            jax.ShapeDtypeStruct((1, 256), F32),
+            jax.ShapeDtypeStruct((ZB, 16, 2, 128), F32),
+            jax.ShapeDtypeStruct((1, 2, 128), F32),
         ),
         in_specs=[VMEM],
         out_specs=(VMEM,) * 2,
@@ -242,7 +241,8 @@
     sub = lax.broadcasted_iota(jnp.int32, (128, size), 0)
     weights = seed_ref[...].astype(F32) * 0.0625
     weight_rows = jnp.where(sub == 1, jnp.broadcast_to(weights, (128, size)), 0.0).astype(BF16)
-    back_rows = jnp.where(sub == 0, jnp.broadcast_to(back_ref[...], (128, size)), 0.0)
+    back = jnp.concatenate([back_ref[0:1, :], back_ref[1:2, :]], axis=1)
+    back_rows = jnp.where(sub == 0, jnp.broadcast_to(back, (128, size)), 0.0)
     eye = (
         lax.broadcasted_iota(jnp.int32, (size, size), 0)
         == lax.broadcasted_iota(jnp.int32, (size, size), 1)
@@ -280,9 +280,7 @@
                 halves[h] = jnp.where(inside, unit, halves[h])
             pivot = spread_row(cols[base, base // 8], 0)
             for j in range(base, base + 16):
-                inverse = pl.reciprocal(pivot, approx=True)
-                for _ in range(2):
-                    inverse = inverse * (2.0 - pivot * inverse)
+                inverse = 1.0 / pivot
                 here = j // 8
                 scales[here] = jnp.where(half_row == j % 8, pivot, scales[here])
                 if j + 1 == NB:
@@ -426,11 +424,11 @@
     drawn = share(sample_rows.reshape(1, 16), ROWS, SOURCES)
     mixed, back = mix(target.reshape(1, height), rademacher.reshape(1, height), design)
     near = pick(position, drawn, mixed.reshape(height, 2, 128), back.reshape(4, 2, 128))
-    pieces = deal(exchange(near.reshape(ZA * Y, 264, 128), NEAR))
+    pieces = deal(exchange(near, NEAR))
     rows, back = fold(exchange(pieces, FAR))
-    rows = exchange(rows, FAR).reshape(ZB * 32, 128)
+    rows = exchange(rows.reshape(ZB, 32, 128), FAR).reshape(ZB * 32, 128)
     images, direction, checksum = factor(
-        exchange(gram(rows), NEAR), back, checksum_seeds.reshape(1, breadth), design
+        exchange(gram(rows), NEAR), back.reshape(2, 128), checksum_seeds.reshape(1, breadth), design
     )
     image, energy = merge(exchange(images, GRPS))
     solved, residual = finish(

time: 144 us -> 142 us (0.986)
  no operation moved by 1% of the time
where the time goes in v1:
time: 142 us
  blocking collectives  96 us (68%)
  starting transfers between devices  19.3 us (14%)
  Pallas kernels  12.7 us (9%)
  waiting for transfers between devices  9 us (6%)
  local copies, waits for them, and re-layouts  4.28 us (3%)
    all_to_all x6, blocking collectives, exchange(): return lax.all_to_all(pieces, axes, split_axis=0, concat_axis=0, tiled=True)  96 us
    all_to_all x1, starting transfers between devices, exchange(): return lax.all_to_all(pieces, axes, split_axis=0, concat_axis=0, tiled=True)  19.3 us
    all_to_all x1, waiting for transfers between devices, exchange(): return lax.all_to_all(pieces, axes, split_axis=0, concat_axis=0, tiled=True)  9 us
    pallas_call x1, Pallas kernels, factor(): pl.pallas_call(factor_kernel, out_shape=(jax.ShapeDtypeStruct((X * C, hei...  7.18 us
    unnamed x12, local copies, waits for them, and re-layouts  3 us
  transfers between devices with their start and end apart: 1, of which 1 were waited for; matrix products, arithmetic and copies ran while one was open for 0% of the time, Pallas kernels for 1%

profile of v1, /device:TPU:1, one launch (start us, length us, event | category | flops | bytes accessed | tf_op | source)
XLA Modules:
  0.0 142.0 jit_solution(17887237766248333089)
XLA Ops:
  0.6 1.3 broadcast_in_dim.8
  1.9 19.3 %all-to-all-start = ((s32[64,1,16]{2,1,0:T(1,128)}), s32[64,1,16]{2,1,0:T(1,128)S(1)}, u32[]{:S(2)}, u32[]{:S(2)}) async-start(s32[64,1,16]{2,1,0:T(1,128)} %broadcast_in_dim.8), calls=%async_computation | async-start | bytes 65536 | tf_op jit(solution)/shard_map/all_to_all | solution.py:128
  21.2 0.0 copy-start
  21.2 1.6 %copy-done = f32[2048,256]{1,0:T(8,128)S(1)} copy-done((f32[2048,256]{1,0:T(8,128)S(1)}, f32[2048,256]{1,0:T(8,128)}, u32[]{:S(2)}) %copy-start) | copy-done | bytes 2097176
  22.8 0.7 copy-done.2
  23.5 0.7 copy-done.5
  24.2 1.6 %mix.1 = (f32[4096,128]{1,0:T(8,128)S(1)}, f32[8,128]{1,0:T(8,128)S(1)}) custom-call(f32[1,2048]{1,0:T(1,128)S(1)} %bitcast.17, s32[1,2048]{1,0:T(1,128)S(1)} %bitcast.22, f32[2048,256]{1,0:T(8,128)S(1)} %copy-done), custom_call_target="tpu_custom_call" | custom-call | flops 1073741824 | bytes 8388608 | tf_op jit(solution)/shard_map/mix/pallas_call | solution.py:80
  25.8 9.0 %all-to-all-done.idx_ref = s32[64,1,16]{2,1,0:T(1,128)S(1)} async-done(((s32[64,1,16]{2,1,0:T(1,128)}), s32[64,1,16]{2,1,0:T(1,128)S(1)}, u32[]{:S(2)}, u32[]{:S(2)}) %all-to-all-start) | async-done | bytes 4128 | tf_op jit(solution)/shard_map/all_to_all | solution.py:128
  34.8 2.4 %pick.1 = f32[8,129,2,128]{3,2,1,0:T(2,128)S(1)} custom-call(s32[1]{0:T(128)} %bitcast.pos_ref, s32[64,1,16]{2,1,0:T(1,128)S(1)} %all-to-all-done.idx_ref, f32[2048,2,128]{2,1,0:T(2,128)S(1)} %bitcast.14, f32[4,2,128]{2,1,0:T(2,128)S(1)} %bitcast.19), custom_call_target="tpu_custom_call" | custom-call | flops 1048576 | bytes 2097152 | tf_op jit(solution)/shard_map/pick/pallas_call | solution.py:116
  37.2 16.2 %all_to_all.35.parts_ref = f32[8,129,2,128]{3,2,1,0:T(2,128)S(1)} all-to-all(f32[8,129,2,128]{3,2,1,0:T(2,128)S(1)} %pick.1), channel_id=1, replica_groups=mesh['zb'=8,'za'=2,'y'=4,'x'=4,'c'=2] {'za','y'}, dimensions={0} | all-to-all | bytes 2113536 | tf_op jit(solution)/shard_map/all_to_all | solution.py:128
  53.5 0.3 deal.1
  53.8 17.3 %all_to_all.36.parts_ref = f32[8,17,2,128]{3,2,1,0:T(2,128)S(1)} all-to-all(f32[8,17,2,128]{3,2,1,0:T(2,128)S(1)} %deal.1), channel_id=1, replica_groups=mesh['zb'=8,'za'=2,'y'=4,'x'=4,'c'=2] {'zb'}, dimensions={0} | all-to-all | bytes 278528 | tf_op jit(solution)/shard_map/all_to_all | solution.py:128
  71.1 0.1 fold.1
  71.1 15.4 %all_to_all.37 = f32[8,32,128]{2,1,0:T(8,128)S(1)} all-to-all(f32[8,32,128]{2,1,0:T(8,128)S(1)} %bitcast.16), channel_id=1, replica_groups=mesh['zb'=8,'za'=2,'y'=4,'x'=4,'c'=2] {'zb'}, dimensions={0} | all-to-all | bytes 262144 | tf_op jit(solution)/shard_map/all_to_all | solution.py:128
  86.5 0.3 gram.1
  86.9 0.0 copy-start.1
  86.9 0.0 copy-start.4
  86.9 15.0 %all_to_all.38.gram_ref = f32[8,264,128]{2,1,0:T(8,128)S(1)} all-to-all(f32[8,264,128]{2,1,0:T(8,128)S(1)} %gram.1), channel_id=1, replica_groups=mesh['zb'=8,'za'=2,'y'=4,'x'=4,'c'=2] {'za','y'}, dimensions={0} | all-to-all | bytes 2162688 | tf_op jit(solution)/shard_map/all_to_all | solution.py:128
  101.9 0.0 copy-done.1
  101.9 7.2 %factor.1 = (f32[8,24,128]{2,1,0:T(8,128)S(1)}, f32[1,256]{1,0:T(1,128)S(1)}, f32[1,256]{1,0:T(1,128)}) custom-call(f32[8,264,128]{2,1,0:T(8,128)S(1)} %all_to_all.38.gram_ref, f32[2,128]{1,0:T(2,128)S(1)} %bitcast.21, s32[1,256]{1,0:T(1,128)S(1)} %bitcast.20, f32[2048,256]{1,0:T(8,128)S(1)} %copy-done.1), custom_call_target="tpu_custom_call" | custom-call | flops 536870912 | bytes 4194304 | tf_op jit(solution)/shard_map/factor/pallas_call | solution.py:362
  109.1 14.8 %all_to_all.39.parts_ref = f32[8,24,128]{2,1,0:T(8,128)S(1)} all-to-all(f32[8,24,128]{2,1,0:T(8,128)S(1)} %get-tuple-element.18), channel_id=1, replica_groups=mesh['zb'=8,'za'=2,'y'=4,'x'=4,'c'=2] {'x','c'}, dimensions={0} | all-to-all | bytes 196608 | tf_op jit(solution)/shard_map/all_to_all | solution.py:128
  123.8 0.1 merge.1
  124.0 17.4 %all_to_all.40.energy_ref = f32[64,1,128]{2,1,0:T(1,128)S(1)} all-to-all(f32[64,1,128]{2,1,0:T(1,128)S(1)} %get-tuple-element.19), channel_id=1, replica_groups=mesh['zb'=8,'za'=2,'y'=4,'x'=4,'c'=2] {'zb','za','y'}, dimensions={0} | all-to-all | bytes 65536 | tf_op jit(solution)/shard_map/all_to_all | solution.py:128
  141.3 0.7 finish.1
  (5 shorter events, 0.0 us)
Async XLA Ops:
  1.9 32.9 %all-to-all-start = ((s32[64,1,16]{2,1,0:T(1,128)}), s32[64,1,16]{2,1,0:T(1,128)S(1)}, u32[]{:S(2)}, u32[]{:S(2)}) async-start(s32[64,1,16]{2,1,0:T(1,128)} %broadcast_in_dim.8), calls=%async_computation | async-start | bytes 65536 | tf_op jit(solution)/shard_map/all_to_all | solution.py:128
  21.2 1.6 %copy-start = (f32[2048,256]{1,0:T(8,128)S(1)}, f32[2048,256]{1,0:T(8,128)}, u32[]{:S(2)}) copy-start(f32[2048,256]{1,0:T(8,128)} %slab_ref.3) | copy-start | bytes 6291460
  22.8 0.7 copy-start.2
  23.5 0.7 copy-start.5
  86.9 15.0 %copy-start.1 = (f32[2048,256]{1,0:T(8,128)S(1)}, f32[2048,256]{1,0:T(8,128)}, u32[]{:S(2)}) copy-start(f32[2048,256]{1,0:T(8,128)} %slab_ref.3) | copy-start | bytes 6291460
  86.9 15.0 %copy-start.4 = (s32[256]{0:T(256)S(1)}, s32[256]{0:T(256)}, u32[]{:S(2)}) copy-start(s32[256]{0:T(256)} %param.9) | copy-start | bytes 3076
  101.9 39.5 %copy-start.3 = (f32[2048]{0:T(1024)S(1)}, f32[2048]{0:T(1024)}, u32[]{:S(2)}) copy-start(f32[2048]{0:T(1024)} %param.7) | copy-start | bytes 24580

commit v2 on v1

--- a/solution.py
+++ b/solution.py
@@ -278,33 +278,53 @@
                 unit = (wide_half - begin == half_row[:, :1] + (8 * h - base)).astype(F32)
                 inside = (wide_half >= begin) & (wide_half < begin + 16)
                 halves[h] = jnp.where(inside, unit, halves[h])
-            pivot = spread_row(cols[base, base // 8], 0)
-            for j in range(base, base + 16):
-                inverse = 1.0 / pivot
-                here = j // 8
-                scales[here] = jnp.where(half_row == j % 8, pivot, scales[here])
-                if j + 1 == NB:
-                    break
-                across = {
-                    c: spread_row(cols[j, c // 8], c % 8) for c in range(j + 1, base + 16)
-                }
-                if j + 1 < base + 16:
-                    pivot = (
-                        spread_row(cols[j + 1, (j + 1) // 8], (j + 1) % 8)
-                        - across[j + 1] * across[j + 1] * inverse
-                    )
+
+            def entry(i, j):
+                return spread_row(cols[j, i // 8], i % 8)
+
+            guards = {
+                j: pl.reciprocal(entry(j, j), approx=True) for j in range(base, base + 16, 2)
+            }
+            first = [entry(base, base), entry(base + 1, base), entry(base + 1, base + 1)]
+            for j in range(base, base + 16, 2):
+                k, here = j + 1, j // 8
+                aa, ab, bb = first
+                part = aa * guards[j]
+                scaled = bb * part - ab * (ab * guards[j])
+                inverse = 1.0 / aa
+                second = part * (1.0 / scaled)
+                slope = ab * inverse
+                scales[here] = jnp.where(half_row == j % 8, inverse, scales[here])
+                scales[here] = jnp.where(half_row == k % 8, second, scales[here])
+                later = range(k + 1, base + 16)
+                left = {c: entry(c, j) for c in later}
+                down = {c: entry(c, k) - slope * left[c] for c in later}
+                if k + 1 < base + 16:
+                    m, n = k + 1, k + 2
+                    first = [
+                        (entry(q, p) - left[p] * left[q] * inverse) - down[p] * down[q] * second
+                        for p, q in ((m, m), (m, n), (n, n))
+                    ]
+                left = {c: left[c] * inverse for c in later}
+                down = {c: down[c] * second for c in later}
                 source = jnp.tile(inverse, (1, tiles)) * spread_row(halves[here], j % 8)
-                for h in range((j + 1) // 8, half_count):
+                other = spread_row(halves[here], k % 8) - jnp.tile(ab, (1, tiles)) * source
+                other = jnp.tile(second, (1, tiles)) * other
+                for h in range(here, half_count):
                     below = cols[j, h]
                     if h == here:
                         below = jnp.where(half_row > j % 8, below, 0.0)
+                    lower = cols[k, h] - below * slope
+                    if h == here:
+                        lower = jnp.where(half_row > k % 8, lower, 0.0)
                     halves[h] = halves[h] - jnp.tile(below, (1, tiles)) * source
-                    for c in range(j + 1, base + 16):
+                    halves[h] = halves[h] - jnp.tile(lower, (1, tiles)) * other
+                    for c in later:
                         if c // 8 <= h:
-                            cols[c, h] = cols[c, h] - below * (across[c] * inverse)
+                            cols[c, h] = cols[c, h] - below * left[c] - lower * down[c]
         panel = jnp.concatenate(
             [
-                half * jnp.tile(lax.rsqrt(scale), (1, tiles))
+                half * jnp.tile(jnp.sqrt(scale), (1, tiles))
                 for half, scale in zip(halves, scales)
             ],
             axis=0,

time: 142 us -> 143 us (level)
  no operation moved by 1% of the time
where the time goes in v2:
time: 143 us
  blocking collectives  96 us (67%)
  starting transfers between devices  19.3 us (13%)
  Pallas kernels  13.6 us (10%)
  waiting for transfers between devices  9 us (6%)
  local copies, waits for them, and re-layouts  4.28 us (3%)
    all_to_all x6, blocking collectives, exchange(): return lax.all_to_all(pieces, axes, split_axis=0, concat_axis=0, tiled=True)  96 us
    all_to_all x1, starting transfers between devices, exchange(): return lax.all_to_all(pieces, axes, split_axis=0, concat_axis=0, tiled=True)  19.3 us
    all_to_all x1, waiting for transfers between devices, exchange(): return lax.all_to_all(pieces, axes, split_axis=0, concat_axis=0, tiled=True)  9 us
    pallas_call x1, Pallas kernels, factor(): pl.pallas_call(factor_kernel, out_shape=(jax.ShapeDtypeStruct((X * C, hei...  8.11 us
    unnamed x12, local copies, waits for them, and re-layouts  3 us
  transfers between devices with their start and end apart: 1, of which 1 were waited for; matrix products, arithmetic and copies ran while one was open for 0% of the time, Pallas kernels for 1%

profile of v2, /device:TPU:1, one launch (start us, length us, event | category | flops | bytes accessed | tf_op | source)
XLA Modules:
  0.0 142.9 jit_solution(2826076693330239532)
XLA Ops:
  0.6 1.3 broadcast_in_dim.8
  1.9 19.3 %all-to-all-start = ((s32[64,1,16]{2,1,0:T(1,128)}), s32[64,1,16]{2,1,0:T(1,128)S(1)}, u32[]{:S(2)}, u32[]{:S(2)}) async-start(s32[64,1,16]{2,1,0:T(1,128)} %broadcast_in_dim.8), calls=%async_computation | async-start | bytes 65536 | tf_op jit(solution)/shard_map/all_to_all | solution.py:128
  21.2 0.0 copy-start
  21.2 1.6 %copy-done = f32[2048,256]{1,0:T(8,128)S(1)} copy-done((f32[2048,256]{1,0:T(8,128)S(1)}, f32[2048,256]{1,0:T(8,128)}, u32[]{:S(2)}) %copy-start) | copy-done | bytes 2097176
  22.8 0.7 copy-done.2
  23.5 0.7 copy-done.5
  24.2 1.6 %mix.1 = (f32[4096,128]{1,0:T(8,128)S(1)}, f32[8,128]{1,0:T(8,128)S(1)}) custom-call(f32[1,2048]{1,0:T(1,128)S(1)} %bitcast.17, s32[1,2048]{1,0:T(1,128)S(1)} %bitcast.22, f32[2048,256]{1,0:T(8,128)S(1)} %copy-done), custom_call_target="tpu_custom_call" | custom-call | flops 1073741824 | bytes 8388608 | tf_op jit(solution)/shard_map/mix/pallas_call | solution.py:80
  25.8 9.0 %all-to-all-done.idx_ref = s32[64,1,16]{2,1,0:T(1,128)S(1)} async-done(((s32[64,1,16]{2,1,0:T(1,128)}), s32[64,1,16]{2,1,0:T(1,128)S(1)}, u32[]{:S(2)}, u32[]{:S(2)}) %all-to-all-start) | async-done | bytes 4128 | tf_op jit(solution)/shard_map/all_to_all | solution.py:128
  34.8 2.4 %pick.1 = f32[8,129,2,128]{3,2,1,0:T(2,128)S(1)} custom-call(s32[1]{0:T(128)} %bitcast.pos_ref, s32[64,1,16]{2,1,0:T(1,128)S(1)} %all-to-all-done.idx_ref, f32[2048,2,128]{2,1,0:T(2,128)S(1)} %bitcast.14, f32[4,2,128]{2,1,0:T(2,128)S(1)} %bitcast.19), custom_call_target="tpu_custom_call" | custom-call | flops 1048576 | bytes 2097152 | tf_op jit(solution)/shard_map/pick/pallas_call | solution.py:116
  37.2 16.2 %all_to_all.35.parts_ref = f32[8,129,2,128]{3,2,1,0:T(2,128)S(1)} all-to-all(f32[8,129,2,128]{3,2,1,0:T(2,128)S(1)} %pick.1), channel_id=1, replica_groups=mesh['zb'=8,'za'=2,'y'=4,'x'=4,'c'=2] {'za','y'}, dimensions={0} | all-to-all | bytes 2113536 | tf_op jit(solution)/shard_map/all_to_all | solution.py:128
  53.5 0.3 deal.1
  53.8 17.3 %all_to_all.36.parts_ref = f32[8,17,2,128]{3,2,1,0:T(2,128)S(1)} all-to-all(f32[8,17,2,128]{3,2,1,0:T(2,128)S(1)} %deal.1), channel_id=1, replica_groups=mesh['zb'=8,'za'=2,'y'=4,'x'=4,'c'=2] {'zb'}, dimensions={0} | all-to-all | bytes 278528 | tf_op jit(solution)/shard_map/all_to_all | solution.py:128
  71.1 0.1 fold.1
  71.1 15.4 %all_to_all.37 = f32[8,32,128]{2,1,0:T(8,128)S(1)} all-to-all(f32[8,32,128]{2,1,0:T(8,128)S(1)} %bitcast.16), channel_id=1, replica_groups=mesh['zb'=8,'za'=2,'y'=4,'x'=4,'c'=2] {'zb'}, dimensions={0} | all-to-all | bytes 262144 | tf_op jit(solution)/shard_map/all_to_all | solution.py:128
  86.5 0.3 gram.1
  86.9 0.0 copy-start.1
  86.9 0.0 copy-start.4
  86.9 15.0 %all_to_all.38.gram_ref = f32[8,264,128]{2,1,0:T(8,128)S(1)} all-to-all(f32[8,264,128]{2,1,0:T(8,128)S(1)} %gram.1), channel_id=1, replica_groups=mesh['zb'=8,'za'=2,'y'=4,'x'=4,'c'=2] {'za','y'}, dimensions={0} | all-to-all | bytes 2162688 | tf_op jit(solution)/shard_map/all_to_all | solution.py:128
  101.9 0.0 copy-done.1
  101.9 8.1 %factor.1 = (f32[8,24,128]{2,1,0:T(8,128)S(1)}, f32[1,256]{1,0:T(1,128)S(1)}, f32[1,256]{1,0:T(1,128)}) custom-call(f32[8,264,128]{2,1,0:T(8,128)S(1)} %all_to_all.38.gram_ref, f32[2,128]{1,0:T(2,128)S(1)} %bitcast.21, s32[1,256]{1,0:T(1,128)S(1)} %bitcast.20, f32[2048,256]{1,0:T(8,128)S(1)} %copy-done.1), custom_call_target="tpu_custom_call" | custom-call | flops 536870912 | bytes 4194304 | tf_op jit(solution)/shard_map/factor/pallas_call | solution.py:382
  110.0 14.7 %all_to_all.39.parts_ref = f32[8,24,128]{2,1,0:T(8,128)S(1)} all-to-all(f32[8,24,128]{2,1,0:T(8,128)S(1)} %get-tuple-element.18), channel_id=1, replica_groups=mesh['zb'=8,'za'=2,'y'=4,'x'=4,'c'=2] {'x','c'}, dimensions={0} | all-to-all | bytes 196608 | tf_op jit(solution)/shard_map/all_to_all | solution.py:128
  124.7 0.1 merge.1
  124.8 17.4 %all_to_all.40.energy_ref = f32[64,1,128]{2,1,0:T(1,128)S(1)} all-to-all(f32[64,1,128]{2,1,0:T(1,128)S(1)} %get-tuple-element.19), channel_id=1, replica_groups=mesh['zb'=8,'za'=2,'y'=4,'x'=4,'c'=2] {'zb','za','y'}, dimensions={0} | all-to-all | bytes 65536 | tf_op jit(solution)/shard_map/all_to_all | solution.py:128
  142.2 0.7 finish.1
  (5 shorter events, 0.0 us)
Async XLA Ops:
  1.9 32.9 %all-to-all-start = ((s32[64,1,16]{2,1,0:T(1,128)}), s32[64,1,16]{2,1,0:T(1,128)S(1)}, u32[]{:S(2)}, u32[]{:S(2)}) async-start(s32[64,1,16]{2,1,0:T(1,128)} %broadcast_in_dim.8), calls=%async_computation | async-start | bytes 65536 | tf_op jit(solution)/shard_map/all_to_all | solution.py:128
  21.2 1.6 %copy-start = (f32[2048,256]{1,0:T(8,128)S(1)}, f32[2048,256]{1,0:T(8,128)}, u32[]{:S(2)}) copy-start(f32[2048,256]{1,0:T(8,128)} %slab_ref.3) | copy-start | bytes 6291460
  22.8 0.7 copy-start.2
  23.5 0.7 copy-start.5
  86.9 15.0 %copy-start.1 = (f32[2048,256]{1,0:T(8,128)S(1)}, f32[2048,256]{1,0:T(8,128)}, u32[]{:S(2)}) copy-start(f32[2048,256]{1,0:T(8,128)} %slab_ref.3) | copy-start | bytes 6291460
  86.9 15.0 %copy-start.4 = (s32[256]{0:T(256)S(1)}, s32[256]{0:T(256)}, u32[]{:S(2)}) copy-start(s32[256]{0:T(256)} %param.9) | copy-start | bytes 3076
  101.9 40.3 %copy-start.3 = (f32[2048]{0:T(1024)S(1)}, f32[2048]{0:T(1024)}, u32[]{:S(2)}) copy-start(f32[2048]{0:T(1024)} %param.7) | copy-start | bytes 24580

commit v3 on v1

--- a/solution.py
+++ b/solution.py
@@ -293,15 +293,15 @@
                         spread_row(cols[j + 1, (j + 1) // 8], (j + 1) % 8)
                         - across[j + 1] * across[j + 1] * inverse
                     )
-                source = jnp.tile(inverse, (1, tiles)) * spread_row(halves[here], j % 8)
+                source = spread_row(halves[here], j % 8)
                 for h in range((j + 1) // 8, half_count):
-                    below = cols[j, h]
+                    below = cols[j, h] * inverse
                     if h == here:
                         below = jnp.where(half_row > j % 8, below, 0.0)
                     halves[h] = halves[h] - jnp.tile(below, (1, tiles)) * source
                     for c in range(j + 1, base + 16):
                         if c // 8 <= h:
-                            cols[c, h] = cols[c, h] - below * (across[c] * inverse)
+                            cols[c, h] = cols[c, h] - below * across[c]
         panel = jnp.concatenate(
             [
                 half * jnp.tile(lax.rsqrt(scale), (1, tiles))

time: 142 us -> 142 us (level)
  no operation moved by 1% of the time
where the time goes in v3:
time: 142 us
  blocking collectives  96 us (68%)
  starting transfers between devices  19.3 us (14%)
  Pallas kernels  12.6 us (9%)
  waiting for transfers between devices  9 us (6%)
  local copies, waits for them, and re-layouts  4.28 us (3%)
    all_to_all x6, blocking collectives, exchange(): return lax.all_to_all(pieces, axes, split_axis=0, concat_axis=0, tiled=True)  96 us
    all_to_all x1, starting transfers between devices, exchange(): return lax.all_to_all(pieces, axes, split_axis=0, concat_axis=0, tiled=True)  19.3 us
    all_to_all x1, waiting for transfers between devices, exchange(): return lax.all_to_all(pieces, axes, split_axis=0, concat_axis=0, tiled=True)  9 us
    pallas_call x1, Pallas kernels, factor(): pl.pallas_call(factor_kernel, out_shape=(jax.ShapeDtypeStruct((X * C, hei...  7.04 us
    unnamed x12, local copies, waits for them, and re-layouts  3 us
  transfers between devices with their start and end apart: 1, of which 1 were waited for; matrix products, arithmetic and copies ran while one was open for 0% of the time, Pallas kernels for 1%

profile of v3, /device:TPU:1, one launch (start us, length us, event | category | flops | bytes accessed | tf_op | source)
XLA Modules:
  0.0 141.8 jit_solution(8718214104045626800)
XLA Ops:
  0.6 1.3 broadcast_in_dim.8
  1.9 19.3 %all-to-all-start = ((s32[64,1,16]{2,1,0:T(1,128)}), s32[64,1,16]{2,1,0:T(1,128)S(1)}, u32[]{:S(2)}, u32[]{:S(2)}) async-start(s32[64,1,16]{2,1,0:T(1,128)} %broadcast_in_dim.8), calls=%async_computation | async-start | bytes 65536 | tf_op jit(solution)/shard_map/all_to_all | solution.py:128
  21.2 0.0 copy-start
  21.2 1.6 %copy-done = f32[2048,256]{1,0:T(8,128)S(1)} copy-done((f32[2048,256]{1,0:T(8,128)S(1)}, f32[2048,256]{1,0:T(8,128)}, u32[]{:S(2)}) %copy-start) | copy-done | bytes 2097176
  22.8 0.7 copy-done.2
  23.5 0.7 copy-done.5
  24.2 1.6 %mix.1 = (f32[4096,128]{1,0:T(8,128)S(1)}, f32[8,128]{1,0:T(8,128)S(1)}) custom-call(f32[1,2048]{1,0:T(1,128)S(1)} %bitcast.17, s32[1,2048]{1,0:T(1,128)S(1)} %bitcast.22, f32[2048,256]{1,0:T(8,128)S(1)} %copy-done), custom_call_target="tpu_custom_call" | custom-call | flops 1073741824 | bytes 8388608 | tf_op jit(solution)/shard_map/mix/pallas_call | solution.py:80
  25.8 9.0 %all-to-all-done.idx_ref = s32[64,1,16]{2,1,0:T(1,128)S(1)} async-done(((s32[64,1,16]{2,1,0:T(1,128)}), s32[64,1,16]{2,1,0:T(1,128)S(1)}, u32[]{:S(2)}, u32[]{:S(2)}) %all-to-all-start) | async-done | bytes 4128 | tf_op jit(solution)/shard_map/all_to_all | solution.py:128
  34.8 2.4 %pick.1 = f32[8,129,2,128]{3,2,1,0:T(2,128)S(1)} custom-call(s32[1]{0:T(128)} %bitcast.pos_ref, s32[64,1,16]{2,1,0:T(1,128)S(1)} %all-to-all-done.idx_ref, f32[2048,2,128]{2,1,0:T(2,128)S(1)} %bitcast.14, f32[4,2,128]{2,1,0:T(2,128)S(1)} %bitcast.19), custom_call_target="tpu_custom_call" | custom-call | flops 1048576 | bytes 2097152 | tf_op jit(solution)/shard_map/pick/pallas_call | solution.py:116
  37.2 16.2 %all_to_all.35.parts_ref = f32[8,129,2,128]{3,2,1,0:T(2,128)S(1)} all-to-all(f32[8,129,2,128]{3,2,1,0:T(2,128)S(1)} %pick.1), channel_id=1, replica_groups=mesh['zb'=8,'za'=2,'y'=4,'x'=4,'c'=2] {'za','y'}, dimensions={0} | all-to-all | bytes 2113536 | tf_op jit(solution)/shard_map/all_to_all | solution.py:128
  53.5 0.3 deal.1
  53.8 17.3 %all_to_all.36.parts_ref = f32[8,17,2,128]{3,2,1,0:T(2,128)S(1)} all-to-all(f32[8,17,2,128]{3,2,1,0:T(2,128)S(1)} %deal.1), channel_id=1, replica_groups=mesh['zb'=8,'za'=2,'y'=4,'x'=4,'c'=2] {'zb'}, dimensions={0} | all-to-all | bytes 278528 | tf_op jit(solution)/shard_map/all_to_all | solution.py:128
  71.1 0.1 fold.1
  71.1 15.4 %all_to_all.37 = f32[8,32,128]{2,1,0:T(8,128)S(1)} all-to-all(f32[8,32,128]{2,1,0:T(8,128)S(1)} %bitcast.16), channel_id=1, replica_groups=mesh['zb'=8,'za'=2,'y'=4,'x'=4,'c'=2] {'zb'}, dimensions={0} | all-to-all | bytes 262144 | tf_op jit(solution)/shard_map/all_to_all | solution.py:128
  86.5 0.3 gram.1
  86.9 0.0 copy-start.1
  86.9 0.0 copy-start.4
  86.9 15.0 %all_to_all.38.gram_ref = f32[8,264,128]{2,1,0:T(8,128)S(1)} all-to-all(f32[8,264,128]{2,1,0:T(8,128)S(1)} %gram.1), channel_id=1, replica_groups=mesh['zb'=8,'za'=2,'y'=4,'x'=4,'c'=2] {'za','y'}, dimensions={0} | all-to-all | bytes 2162688 | tf_op jit(solution)/shard_map/all_to_all | solution.py:128
  101.9 0.0 copy-done.4
  101.9 7.0 %factor.1 = (f32[8,24,128]{2,1,0:T(8,128)S(1)}, f32[1,256]{1,0:T(1,128)S(1)}, f32[1,256]{1,0:T(1,128)}) custom-call(f32[8,264,128]{2,1,0:T(8,128)S(1)} %all_to_all.38.gram_ref, f32[2,128]{1,0:T(2,128)S(1)} %bitcast.21, s32[1,256]{1,0:T(1,128)S(1)} %bitcast.20, f32[2048,256]{1,0:T(8,128)S(1)} %copy-done.1), custom_call_target="tpu_custom_call" | custom-call | flops 536870912 | bytes 4194304 | tf_op jit(solution)/shard_map/factor/pallas_call | solution.py:362
  108.9 14.8 %all_to_all.39.parts_ref = f32[8,24,128]{2,1,0:T(8,128)S(1)} all-to-all(f32[8,24,128]{2,1,0:T(8,128)S(1)} %get-tuple-element.18), channel_id=1, replica_groups=mesh['zb'=8,'za'=2,'y'=4,'x'=4,'c'=2] {'x','c'}, dimensions={0} | all-to-all | bytes 196608 | tf_op jit(solution)/shard_map/all_to_all | solution.py:128
  123.7 0.1 merge.1
  123.8 17.4 %all_to_all.40.energy_ref = f32[64,1,128]{2,1,0:T(1,128)S(1)} all-to-all(f32[64,1,128]{2,1,0:T(1,128)S(1)} %get-tuple-element.19), channel_id=1, replica_groups=mesh['zb'=8,'za'=2,'y'=4,'x'=4,'c'=2] {'zb','za','y'}, dimensions={0} | all-to-all | bytes 65536 | tf_op jit(solution)/shard_map/all_to_all | solution.py:128
  141.2 0.7 finish.1
  (5 shorter events, 0.0 us)
Async XLA Ops:
  1.9 32.9 %all-to-all-start = ((s32[64,1,16]{2,1,0:T(1,128)}), s32[64,1,16]{2,1,0:T(1,128)S(1)}, u32[]{:S(2)}, u32[]{:S(2)}) async-start(s32[64,1,16]{2,1,0:T(1,128)} %broadcast_in_dim.8), calls=%async_computation | async-start | bytes 65536 | tf_op jit(solution)/shard_map/all_to_all | solution.py:128
  21.2 1.6 %copy-start = (f32[2048,256]{1,0:T(8,128)S(1)}, f32[2048,256]{1,0:T(8,128)}, u32[]{:S(2)}) copy-start(f32[2048,256]{1,0:T(8,128)} %slab_ref.3) | copy-start | bytes 6291460
  22.8 0.7 copy-start.2
  23.5 0.7 copy-start.5
  86.9 15.0 %copy-start.1 = (f32[2048,256]{1,0:T(8,128)S(1)}, f32[2048,256]{1,0:T(8,128)}, u32[]{:S(2)}) copy-start(f32[2048,256]{1,0:T(8,128)} %slab_ref.3) | copy-start | bytes 6291460
  86.9 15.0 %copy-start.4 = (s32[256]{0:T(256)S(1)}, s32[256]{0:T(256)}, u32[]{:S(2)}) copy-start(s32[256]{0:T(256)} %param.9) | copy-start | bytes 3076
  101.9 39.3 %copy-start.3 = (f32[2048]{0:T(1024)S(1)}, f32[2048]{0:T(1024)}, u32[]{:S(2)}) copy-start(f32[2048]{0:T(1024)} %param.7) | copy-start | bytes 24580

commit v4 on v3

--- a/solution.py
+++ b/solution.py
@@ -312,9 +312,12 @@
         work_ref[at : at + NB, :] = panel
         if at + NB < size:
             hi, mid, lo = split3(panel)
-            zero = jnp.zeros((NB, size), BF16)
-            keep = lane[:, :size] >= at + NB
-            lhi, lmid, llo = [jnp.where(keep, term[:, :size], zero) for term in (hi, mid, lo)]
+            begin = 128 if at + NB >= 128 else 0
+            zero = jnp.zeros((NB, size - begin), BF16)
+            keep = lane[:, begin:size] >= at + NB
+            lhi, lmid, llo = [
+                jnp.where(keep, term[:, begin:size], zero) for term in (hi, mid, lo)
+            ]
             left = jnp.concatenate([lhi, lhi, lmid, lhi, llo, lmid], axis=0)
             blank = (row < 16) & (lane >= at + 16) & (lane < at + NB)
             hi, mid, lo = [
@@ -323,10 +326,16 @@
             right = jnp.concatenate([hi, mid, hi, lo, hi, mid], axis=0)
             change = dot_tn(left, right)
             rest = size - at - NB
-            wide_lane = lax.broadcasted_iota(jnp.int32, (rest, wide), 1)
-            old = work_ref[at + NB :, :]
-            old = jnp.where((wide_lane >= at) & (wide_lane < at + NB), 0.0, old)
-            work_ref[at + NB :, :] = old - change[at + NB :, :]
+            tile = at // 128 * 128
+            tile_lane = lax.broadcasted_iota(jnp.int32, (rest, 128), 1) + tile
+            inside = (tile_lane >= at) & (tile_lane < at + NB)
+            for start in range(0, wide, 128):
+                old = work_ref[at + NB :, start : start + 128]
+                if start == tile:
+                    old = jnp.where(inside, 0.0, old)
+                work_ref[at + NB :, start : start + 128] = (
+                    old - change[at + NB - begin :, start : start + 128]
+                )
 
     lower_inv = jnp.where(
         lax.broadcasted_iota(jnp.int32, (size, size), 0)

time: 142 us -> 142 us (level)
  no operation moved by 1% of the time
where the time goes in v4:
time: 142 us
  blocking collectives  96 us (68%)
  starting transfers between devices  19.3 us (14%)
  Pallas kernels  12.4 us (9%)
  waiting for transfers between devices  9 us (6%)
  local copies, waits for them, and re-layouts  4.28 us (3%)
    all_to_all x6, blocking collectives, exchange(): return lax.all_to_all(pieces, axes, split_axis=0, concat_axis=0, tiled=True)  96 us
    all_to_all x1, starting transfers between devices, exchange(): return lax.all_to_all(pieces, axes, split_axis=0, concat_axis=0, tiled=True)  19.3 us
    all_to_all x1, waiting for transfers between devices, exchange(): return lax.all_to_all(pieces, axes, split_axis=0, concat_axis=0, tiled=True)  9 us
    pallas_call x1, Pallas kernels, factor(): pl.pallas_call(factor_kernel, out_shape=(jax.ShapeDtypeStruct((X * C, hei...  6.85 us
    unnamed x12, local copies, waits for them, and re-layouts  3 us
  transfers between devices with their start and end apart: 1, of which 1 were waited for; matrix products, arithmetic and copies ran while one was open for 0% of the time, Pallas kernels for 1%

profile of v4, /device:TPU:1, one launch (start us, length us, event | category | flops | bytes accessed | tf_op | source)
XLA Modules:
  0.0 141.7 jit_solution(5656061632527254250)
XLA Ops:
  0.6 1.3 broadcast_in_dim.8
  1.9 19.3 %all-to-all-start = ((s32[64,1,16]{2,1,0:T(1,128)}), s32[64,1,16]{2,1,0:T(1,128)S(1)}, u32[]{:S(2)}, u32[]{:S(2)}) async-start(s32[64,1,16]{2,1,0:T(1,128)} %broadcast_in_dim.8), calls=%async_computation | async-start | bytes 65536 | tf_op jit(solution)/shard_map/all_to_all | solution.py:128
  21.2 0.0 copy-start
  21.2 1.6 %copy-done = f32[2048,256]{1,0:T(8,128)S(1)} copy-done((f32[2048,256]{1,0:T(8,128)S(1)}, f32[2048,256]{1,0:T(8,128)}, u32[]{:S(2)}) %copy-start) | copy-done | bytes 2097176
  22.8 0.7 copy-done.2
  23.5 0.7 copy-done.5
  24.2 1.6 %mix.1 = (f32[4096,128]{1,0:T(8,128)S(1)}, f32[8,128]{1,0:T(8,128)S(1)}) custom-call(f32[1,2048]{1,0:T(1,128)S(1)} %bitcast.17, s32[1,2048]{1,0:T(1,128)S(1)} %bitcast.22, f32[2048,256]{1,0:T(8,128)S(1)} %copy-done), custom_call_target="tpu_custom_call" | custom-call | flops 1073741824 | bytes 8388608 | tf_op jit(solution)/shard_map/mix/pallas_call | solution.py:80
  25.8 9.0 %all-to-all-done.idx_ref = s32[64,1,16]{2,1,0:T(1,128)S(1)} async-done(((s32[64,1,16]{2,1,0:T(1,128)}), s32[64,1,16]{2,1,0:T(1,128)S(1)}, u32[]{:S(2)}, u32[]{:S(2)}) %all-to-all-start) | async-done | bytes 4128 | tf_op jit(solution)/shard_map/all_to_all | solution.py:128
  34.8 2.4 %pick.1 = f32[8,129,2,128]{3,2,1,0:T(2,128)S(1)} custom-call(s32[1]{0:T(128)} %bitcast.pos_ref, s32[64,1,16]{2,1,0:T(1,128)S(1)} %all-to-all-done.idx_ref, f32[2048,2,128]{2,1,0:T(2,128)S(1)} %bitcast.14, f32[4,2,128]{2,1,0:T(2,128)S(1)} %bitcast.19), custom_call_target="tpu_custom_call" | custom-call | flops 1048576 | bytes 2097152 | tf_op jit(solution)/shard_map/pick/pallas_call | solution.py:116
  37.2 16.2 %all_to_all.35.parts_ref = f32[8,129,2,128]{3,2,1,0:T(2,128)S(1)} all-to-all(f32[8,129,2,128]{3,2,1,0:T(2,128)S(1)} %pick.1), channel_id=1, replica_groups=mesh['zb'=8,'za'=2,'y'=4,'x'=4,'c'=2] {'za','y'}, dimensions={0} | all-to-all | bytes 2113536 | tf_op jit(solution)/shard_map/all_to_all | solution.py:128
  53.5 0.3 deal.1
  53.8 17.3 %all_to_all.36.parts_ref = f32[8,17,2,128]{3,2,1,0:T(2,128)S(1)} all-to-all(f32[8,17,2,128]{3,2,1,0:T(2,128)S(1)} %deal.1), channel_id=1, replica_groups=mesh['zb'=8,'za'=2,'y'=4,'x'=4,'c'=2] {'zb'}, dimensions={0} | all-to-all | bytes 278528 | tf_op jit(solution)/shard_map/all_to_all | solution.py:128
  71.1 0.1 fold.1
  71.1 15.4 %all_to_all.37 = f32[8,32,128]{2,1,0:T(8,128)S(1)} all-to-all(f32[8,32,128]{2,1,0:T(8,128)S(1)} %bitcast.16), channel_id=1, replica_groups=mesh['zb'=8,'za'=2,'y'=4,'x'=4,'c'=2] {'zb'}, dimensions={0} | all-to-all | bytes 262144 | tf_op jit(solution)/shard_map/all_to_all | solution.py:128
  86.5 0.3 gram.1
  86.9 0.0 copy-start.1
  86.9 0.0 copy-start.4
  86.9 15.0 %all_to_all.38.gram_ref = f32[8,264,128]{2,1,0:T(8,128)S(1)} all-to-all(f32[8,264,128]{2,1,0:T(8,128)S(1)} %gram.1), channel_id=1, replica_groups=mesh['zb'=8,'za'=2,'y'=4,'x'=4,'c'=2] {'za','y'}, dimensions={0} | all-to-all | bytes 2162688 | tf_op jit(solution)/shard_map/all_to_all | solution.py:128
  101.9 0.0 copy-done.1
  101.9 6.8 %factor.1 = (f32[8,24,128]{2,1,0:T(8,128)S(1)}, f32[1,256]{1,0:T(1,128)S(1)}, f32[1,256]{1,0:T(1,128)}) custom-call(f32[8,264,128]{2,1,0:T(8,128)S(1)} %all_to_all.38.gram_ref, f32[2,128]{1,0:T(2,128)S(1)} %bitcast.21, s32[1,256]{1,0:T(1,128)S(1)} %bitcast.20, f32[2048,256]{1,0:T(8,128)S(1)} %copy-done.1), custom_call_target="tpu_custom_call" | custom-call | flops 536870912 | bytes 4194304 | tf_op jit(solution)/shard_map/factor/pallas_call | solution.py:371
  108.7 14.8 %all_to_all.39.parts_ref = f32[8,24,128]{2,1,0:T(8,128)S(1)} all-to-all(f32[8,24,128]{2,1,0:T(8,128)S(1)} %get-tuple-element.18), channel_id=1, replica_groups=mesh['zb'=8,'za'=2,'y'=4,'x'=4,'c'=2] {'x','c'}, dimensions={0} | all-to-all | bytes 196608 | tf_op jit(solution)/shard_map/all_to_all | solution.py:128
  123.5 0.1 merge.1
  123.6 17.4 %all_to_all.40.energy_ref = f32[64,1,128]{2,1,0:T(1,128)S(1)} all-to-all(f32[64,1,128]{2,1,0:T(1,128)S(1)} %get-tuple-element.19), channel_id=1, replica_groups=mesh['zb'=8,'za'=2,'y'=4,'x'=4,'c'=2] {'zb','za','y'}, dimensions={0} | all-to-all | bytes 65536 | tf_op jit(solution)/shard_map/all_to_all | solution.py:128
  141.0 0.7 finish.1
  (5 shorter events, 0.0 us)
Async XLA Ops:
  1.9 32.9 %all-to-all-start = ((s32[64,1,16]{2,1,0:T(1,128)}), s32[64,1,16]{2,1,0:T(1,128)S(1)}, u32[]{:S(2)}, u32[]{:S(2)}) async-start(s32[64,1,16]{2,1,0:T(1,128)} %broadcast_in_dim.8), calls=%async_computation | async-start | bytes 65536 | tf_op jit(solution)/shard_map/all_to_all | solution.py:128
  21.2 1.6 %copy-start = (f32[2048,256]{1,0:T(8,128)S(1)}, f32[2048,256]{1,0:T(8,128)}, u32[]{:S(2)}) copy-start(f32[2048,256]{1,0:T(8,128)} %slab_ref.3) | copy-start | bytes 6291460
  22.8 0.7 copy-start.2
  23.5 0.7 copy-start.5
  86.9 15.0 %copy-start.1 = (f32[2048,256]{1,0:T(8,128)S(1)}, f32[2048,256]{1,0:T(8,128)}, u32[]{:S(2)}) copy-start(f32[2048,256]{1,0:T(8,128)} %slab_ref.3) | copy-start | bytes 6291460
  86.9 15.0 %copy-start.4 = (s32[256]{0:T(256)S(1)}, s32[256]{0:T(256)}, u32[]{:S(2)}) copy-start(s32[256]{0:T(256)} %param.9) | copy-start | bytes 3076
  101.9 39.1 %copy-start.3 = (f32[2048]{0:T(1024)S(1)}, f32[2048]{0:T(1024)}, u32[]{:S(2)}) copy-start(f32[2048]{0:T(1024)} %param.7) | copy-start | bytes 24580

commit v5 on v4

--- a/solution.py
+++ b/solution.py
@@ -109,7 +109,7 @@
         out_ref[piece, 128] = back_ref[0]
         return carry
 
-    lax.fori_loop(0, out_ref.shape[0], one, 0)
+    lax.fori_loop(0, out_ref.shape[0], one, 0, unroll=2)
 
 
 def pick(position, drawn, mixed, back):

time: 142 us -> 142 us (level)
  no operation moved by 1% of the time
where the time goes in v5:
time: 142 us
  blocking collectives  96 us (68%)
  starting transfers between devices  19.3 us (14%)
  Pallas kernels  12.4 us (9%)
  waiting for transfers between devices  9 us (6%)
  local copies, waits for them, and re-layouts  4.28 us (3%)
    all_to_all x6, blocking collectives, exchange(): return lax.all_to_all(pieces, axes, split_axis=0, concat_axis=0, tiled=True)  96 us
    all_to_all x1, starting transfers between devices, exchange(): return lax.all_to_all(pieces, axes, split_axis=0, concat_axis=0, tiled=True)  19.3 us
    all_to_all x1, waiting for transfers between devices, exchange(): return lax.all_to_all(pieces, axes, split_axis=0, concat_axis=0, tiled=True)  9 us
    pallas_call x1, Pallas kernels, factor(): pl.pallas_call(factor_kernel, out_shape=(jax.ShapeDtypeStruct((X * C, hei...  6.84 us
    unnamed x12, local copies, waits for them, and re-layouts  3 us
  transfers between devices with their start and end apart: 1, of which 1 were waited for; matrix products, arithmetic and copies ran while one was open for 0% of the time, Pallas kernels for 1%

profile of v5, /device:TPU:1, one launch (start us, length us, event | category | flops | bytes accessed | tf_op | source)
XLA Modules:
  0.0 141.6 jit_solution(7988370019486694184)
XLA Ops:
  0.6 1.3 broadcast_in_dim.8
  1.9 19.3 %all-to-all-start = ((s32[64,1,16]{2,1,0:T(1,128)}), s32[64,1,16]{2,1,0:T(1,128)S(1)}, u32[]{:S(2)}, u32[]{:S(2)}) async-start(s32[64,1,16]{2,1,0:T(1,128)} %broadcast_in_dim.8), calls=%async_computation | async-start | bytes 65536 | tf_op jit(solution)/shard_map/all_to_all | solution.py:128
  21.2 0.0 copy-start
  21.2 1.6 %copy-done = f32[2048,256]{1,0:T(8,128)S(1)} copy-done((f32[2048,256]{1,0:T(8,128)S(1)}, f32[2048,256]{1,0:T(8,128)}, u32[]{:S(2)}) %copy-start) | copy-done | bytes 2097176
  22.8 0.7 copy-done.2
  23.5 0.7 copy-done.5
  24.2 1.6 %mix.1 = (f32[4096,128]{1,0:T(8,128)S(1)}, f32[8,128]{1,0:T(8,128)S(1)}) custom-call(f32[1,2048]{1,0:T(1,128)S(1)} %bitcast.17, s32[1,2048]{1,0:T(1,128)S(1)} %bitcast.22, f32[2048,256]{1,0:T(8,128)S(1)} %copy-done), custom_call_target="tpu_custom_call" | custom-call | flops 1073741824 | bytes 8388608 | tf_op jit(solution)/shard_map/mix/pallas_call | solution.py:80
  25.8 9.0 %all-to-all-done.idx_ref = s32[64,1,16]{2,1,0:T(1,128)S(1)} async-done(((s32[64,1,16]{2,1,0:T(1,128)}), s32[64,1,16]{2,1,0:T(1,128)S(1)}, u32[]{:S(2)}, u32[]{:S(2)}) %all-to-all-start) | async-done | bytes 4128 | tf_op jit(solution)/shard_map/all_to_all | solution.py:128
  34.8 2.4 %pick.1 = f32[8,129,2,128]{3,2,1,0:T(2,128)S(1)} custom-call(s32[1]{0:T(128)} %bitcast.pos_ref, s32[64,1,16]{2,1,0:T(1,128)S(1)} %all-to-all-done.idx_ref, f32[2048,2,128]{2,1,0:T(2,128)S(1)} %bitcast.14, f32[4,2,128]{2,1,0:T(2,128)S(1)} %bitcast.19), custom_call_target="tpu_custom_call" | custom-call | flops 1048576 | bytes 2097152 | tf_op jit(solution)/shard_map/pick/pallas_call | solution.py:116
  37.2 16.2 %all_to_all.35.parts_ref = f32[8,129,2,128]{3,2,1,0:T(2,128)S(1)} all-to-all(f32[8,129,2,128]{3,2,1,0:T(2,128)S(1)} %pick.1), channel_id=1, replica_groups=mesh['zb'=8,'za'=2,'y'=4,'x'=4,'c'=2] {'za','y'}, dimensions={0} | all-to-all | bytes 2113536 | tf_op jit(solution)/shard_map/all_to_all | solution.py:128
  53.4 0.3 deal.1
  53.8 17.3 %all_to_all.36.parts_ref = f32[8,17,2,128]{3,2,1,0:T(2,128)S(1)} all-to-all(f32[8,17,2,128]{3,2,1,0:T(2,128)S(1)} %deal.1), channel_id=1, replica_groups=mesh['zb'=8,'za'=2,'y'=4,'x'=4,'c'=2] {'zb'}, dimensions={0} | all-to-all | bytes 278528 | tf_op jit(solution)/shard_map/all_to_all | solution.py:128
  71.0 0.1 fold.1
  71.1 15.4 %all_to_all.37 = f32[8,32,128]{2,1,0:T(8,128)S(1)} all-to-all(f32[8,32,128]{2,1,0:T(8,128)S(1)} %bitcast.16), channel_id=1, replica_groups=mesh['zb'=8,'za'=2,'y'=4,'x'=4,'c'=2] {'zb'}, dimensions={0} | all-to-all | bytes 262144 | tf_op jit(solution)/shard_map/all_to_all | solution.py:128
  86.5 0.3 gram.1
  86.8 0.0 copy-start.1
  86.9 0.0 copy-start.4
  86.9 15.0 %all_to_all.38.gram_ref = f32[8,264,128]{2,1,0:T(8,128)S(1)} all-to-all(f32[8,264,128]{2,1,0:T(8,128)S(1)} %gram.1), channel_id=1, replica_groups=mesh['zb'=8,'za'=2,'y'=4,'x'=4,'c'=2] {'za','y'}, dimensions={0} | all-to-all | bytes 2162688 | tf_op jit(solution)/shard_map/all_to_all | solution.py:128
  101.8 0.0 copy-done.1
  101.8 6.8 %factor.1 = (f32[8,24,128]{2,1,0:T(8,128)S(1)}, f32[1,256]{1,0:T(1,128)S(1)}, f32[1,256]{1,0:T(1,128)}) custom-call(f32[8,264,128]{2,1,0:T(8,128)S(1)} %all_to_all.38.gram_ref, f32[2,128]{1,0:T(2,128)S(1)} %bitcast.21, s32[1,256]{1,0:T(1,128)S(1)} %bitcast.20, f32[2048,256]{1,0:T(8,128)S(1)} %copy-done.1), custom_call_target="tpu_custom_call" | custom-call | flops 536870912 | bytes 4194304 | tf_op jit(solution)/shard_map/factor/pallas_call | solution.py:371
  108.7 14.8 %all_to_all.39.parts_ref = f32[8,24,128]{2,1,0:T(8,128)S(1)} all-to-all(f32[8,24,128]{2,1,0:T(8,128)S(1)} %get-tuple-element.18), channel_id=1, replica_groups=mesh['zb'=8,'za'=2,'y'=4,'x'=4,'c'=2] {'x','c'}, dimensions={0} | all-to-all | bytes 196608 | tf_op jit(solution)/shard_map/all_to_all | solution.py:128
  123.5 0.1 merge.1
  123.6 17.4 %all_to_all.40.energy_ref = f32[64,1,128]{2,1,0:T(1,128)S(1)} all-to-all(f32[64,1,128]{2,1,0:T(1,128)S(1)} %get-tuple-element.19), channel_id=1, replica_groups=mesh['zb'=8,'za'=2,'y'=4,'x'=4,'c'=2] {'zb','za','y'}, dimensions={0} | all-to-all | bytes 65536 | tf_op jit(solution)/shard_map/all_to_all | solution.py:128
  141.0 0.7 finish.1
  (5 shorter events, 0.0 us)
Async XLA Ops:
  1.9 32.9 %all-to-all-start = ((s32[64,1,16]{2,1,0:T(1,128)}), s32[64,1,16]{2,1,0:T(1,128)S(1)}, u32[]{:S(2)}, u32[]{:S(2)}) async-start(s32[64,1,16]{2,1,0:T(1,128)} %broadcast_in_dim.8), calls=%async_computation | async-start | bytes 65536 | tf_op jit(solution)/shard_map/all_to_all | solution.py:128
  21.2 1.6 %copy-start = (f32[2048,256]{1,0:T(8,128)S(1)}, f32[2048,256]{1,0:T(8,128)}, u32[]{:S(2)}) copy-start(f32[2048,256]{1,0:T(8,128)} %slab_ref.3) | copy-start | bytes 6291460
  22.8 0.7 copy-start.2
  23.5 0.7 copy-start.5
  86.8 15.0 %copy-start.1 = (f32[2048,256]{1,0:T(8,128)S(1)}, f32[2048,256]{1,0:T(8,128)}, u32[]{:S(2)}) copy-start(f32[2048,256]{1,0:T(8,128)} %slab_ref.3) | copy-start | bytes 6291460
  86.9 15.0 %copy-start.4 = (s32[256]{0:T(256)S(1)}, s32[256]{0:T(256)}, u32[]{:S(2)}) copy-start(s32[256]{0:T(256)} %param.9) | copy-start | bytes 3076
  101.8 39.1 %copy-start.3 = (f32[2048]{0:T(1024)S(1)}, f32[2048]{0:T(1024)}, u32[]{:S(2)}) copy-start(f32[2048]{0:T(1024)} %param.7) | copy-start | bytes 24580
